TPU v7x, 512 devices: a whole 4x4x16 slice. The times are simulated.
512 devices in a mesh: dp: 32 (over z_lo, x, core), mp: 16 (over z_hi, y).
Axes of the slice: x: 4, y: 4, z: 16 (z_hi: 4, z_lo: 4; z = z_hi * 4 + z_lo), core: 2. Of those that a mesh axis runs over, the one named last changes fastest.
Arguments:
- grads: bfloat16 [32, 2, 256, 28672], P('dp', None, None, 'mp'), may hold values from -6 to 6
- weights: bfloat16 [2, 256, 28672], P(None, 'dp', 'mp'), may hold values from -1.5 to 1.5
- first_moment: float32 [2, 256, 256], P(None, 'dp'), may hold values from -6 to 6
- second_moment: float32 [2, 256, 256], P(None, 'dp'), may hold values from 1 to 16
- old_seeds: int32 [2], replicated, may hold values from 0 to 999999
- new_seeds: int32 [2], replicated, may hold values from 0 to 999999
Outputs:
- new_weights: bfloat16 [2, 256, 28672], P(None, None, 'mp')
- new_first: float32 [2, 256, 256], P(None, 'dp')
- new_second: float32 [2, 256, 256], P(None, 'dp')
Inputs may be any that keep to these rules, and one draw needn't show every extreme that they name: `old_seeds`: seeds of the counter-based generator; old and new seeds are drawn independently. `new_seeds`: seeds of the counter-based generator; old and new seeds are drawn independently.
All inputs are finite; a program needn't handle non-finite values.
Results may differ from a plain program's by a relative error of at most 0.0053.
Values may be sent and summed in bfloat16 or wider, within the bound.
No kernel may reach another device: no remote copies, remote signals or barrier semaphores. Data moves between devices by JAX's collectives and lax.ppermute only.
A program may use at most 64 MiB of HBM per device.

v0:
```python
import math
import jax
import jax.numpy as jnp
from jax import lax
from jax.sharding import PartitionSpec as P


def scramble(values):
    return (values % 46000 * (values // 2 % 46000 + 1) + 12345) % 65521


def generate(seed_value, rank_ids, columns):
    offset = seed_value % 65521
    row_key = (rank_ids * 251 + offset * 3) % 65521
    col_key = scramble((columns * 7 + offset) % 65521)
    hashed = scramble((row_key[:, None] + 2 * col_key[None, :]) % 65521)
    hashed = scramble((hashed * 3 + row_key[:, None]) % 65521)
    spread = math.sqrt(12.0 / rank_ids.shape[0])
    return ((hashed.astype(jnp.float32) + 0.5) / 65521.0 - 0.5) * spread


def inner_rank(left, right):
    return lax.dot_general(
        left, right, (((1,), (1,)), ((), ())), preferred_element_type=jnp.float32
    )


def shards(grads, weights, first_moment, second_moment, old_seeds, new_seeds):
    layers = weights.shape[0]
    rank = first_moment.shape[2]
    ncols = weights.shape[2]
    col_start = lax.axis_index("mp") * ncols
    columns = col_start + jnp.arange(ncols, dtype=jnp.int32)
    rank_ids = jnp.arange(rank, dtype=jnp.int32)
    new_projs = [
        generate(new_seeds[layer_id], rank_ids, columns).astype(jnp.bfloat16)
        for layer_id in range(layers)
    ]
    gathered = []
    firsts = []
    seconds = []
    for layer_id in range(layers):
        new_proj = new_projs[layer_id]
        old_proj = generate(old_seeds[layer_id], rank_ids, columns).astype(jnp.bfloat16)
        gram_matrix = lax.psum(inner_rank(old_proj, new_proj), "mp")
        partial_value = inner_rank(grads[0, layer_id], new_proj)
        owned = lax.psum_scatter(partial_value, "dp", scatter_dimension=0, tiled=True)
        compressed = lax.psum(owned, "mp")
        moment = (
            0.9 * jnp.dot(first_moment[layer_id], gram_matrix, precision=lax.Precision.HIGHEST)
            + 0.1 * compressed
        )
        second = (
            0.95
            * jnp.dot(
                second_moment[layer_id], gram_matrix * gram_matrix, precision=lax.Precision.HIGHEST
            )
            + 0.05 * compressed * compressed
        )
        direction = (moment / (jnp.sqrt(second) + 1e-08)).astype(jnp.bfloat16)
        update = jnp.dot(direction, new_proj, preferred_element_type=jnp.float32)
        block = (weights[layer_id].astype(jnp.float32) - 0.5 * update).astype(jnp.bfloat16)
        gathered.append(lax.all_gather(block, "dp", axis=0, tiled=True))
        firsts.append(moment)
        seconds.append(second)
    new_weights = jnp.stack(gathered)
    return (new_weights, jnp.stack(firsts), jnp.stack(seconds))


def solution(mesh):
    placed = (
        P("dp", None, None, "mp"),
        P(None, "dp", "mp"),
        P(None, "dp", None),
        P(None, "dp", None),
        P(),
        P(),
    )
    return jax.shard_map(
        shards,
        mesh=mesh,
        in_specs=placed,
        out_specs=(P(None, None, "mp"), P(None, "dp", None), P(None, "dp", None)),
        check_vma=False,
    )
```

profile of v0, /device:TPU:1, one launch (start us, length us, event | category | flops | bytes accessed | tf_op | source)
XLA Modules:
  0.0 542.0 jit_solution(2791521066732754462)
XLA Ops:
  8.0 0.0 reduce-scatter.5.cloned.1.call-start
  8.0 1.3 fusion.313
  10.1 0.0 copy-start.3
  10.1 11.9 %convolution_bitcast_fusion = f32[256,256]{1,0:T(8,128)} fusion(bf16[1,2,256,1792]{3,2,1,0:T(8,128)(2,1)} %param.6, s32[1792]{0:T(1024)S(1)} %fusion.205, s32[256]{0:T(256)S(1)} %and_select_fusion), kind=kOutput, calls=%fused_computation.211 | convolution fusion | flops 277544960 | bytes 1187840 | tf_op jit(solution)/shard_map/dot_general | solution.py:23
  22.0 0.0 reduce-scatter.5.cloned.1.call-update
  22.1 0.3 reduce-scatter.3.cloned.1.call-start
  23.1 0.0 copy-done.3
  23.1 0.0 copy-start.2
  23.1 10.6 %convolution_bitcast_fusion.1 = f32[256,256]{1,0:T(8,128)} fusion(bf16[1,2,256,1792]{3,2,1,0:T(8,128)(2,1)S(1)} %copy-done.3, s32[1792]{0:T(1024)S(1)} %fusion.191, s32[256]{0:T(256)S(1)} %and_select_fusion.2), kind=kOutput, calls=%fused_computation.212 | convolution fusion | flops 277544960 | bytes 1188864 | tf_op jit(solution)/shard_map/dot_general | solution.py:23
  33.7 0.0 reduce-scatter.3.cloned.1.call-update
  33.8 0.4 all-reduce.4.cloned.1.call-start
  34.2 0.0 copy-done.2
  34.2 0.6 fusion.312
  36.1 0.1 fusion.184
  36.2 20.4 %fusion.138 = f32[256,256]{1,0:T(8,128)} fusion(s32[1792]{0:T(1024)S(1)} %fusion.191, s32[256]{0:T(256)S(1)} %and_select_fusion.2, s32[1792]{0:T(1024)S(1)} %get-tuple-element.11, s32[256]{0:T(256)S(1)} %and_select_fusion.3), kind=kOutput, calls=%fused_computation.226 | convolution fusion | flops 320208896 | bytes 278528 | tf_op jit(solution)/shard_map/dot_general | solution.py:23
  56.7 0.0 copy-start
  56.7 0.0 copy-start.1
  56.7 0.0 copy-start.4
  56.7 20.8 %fusion.136 = f32[256,256]{1,0:T(8,128)} fusion(s32[1792]{0:T(1024)S(1)} %get-tuple-element.12, s32[256]{0:T(256)S(1)} %and_select_fusion.1, s32[1792]{0:T(1024)S(1)} %fusion.205, s32[256]{0:T(256)S(1)} %and_select_fusion), kind=kOutput, calls=%fused_computation.225 | convolution fusion | flops 320208896 | bytes 278528 | tf_op jit(solution)/shard_map/dot_general | solution.py:23
  77.5 0.0 all-reduce.4.cloned.1.call-update
  77.5 95.8 %reduce-scatter.5.cloned.1.call-done = f32[8,256]{1,0:T(8,128)} async-done(((f32[256,256]{1,0:T(8,128)}), f32[8,256]{1,0:T(8,128)}) %reduce-scatter.5.cloned.1.call-update) | async-done | bytes 8208 | tf_op jit(solution)/shard_map/reduce_scatter | solution.py:47
  173.4 149.7 %reduce-scatter.3.cloned.1.call-done = f32[8,256]{1,0:T(8,128)} async-done(((f32[256,256]{1,0:T(8,128)}), f32[8,256]{1,0:T(8,128)}) %reduce-scatter.3.cloned.1.call-update) | async-done | bytes 8208 | tf_op jit(solution)/shard_map/reduce_scatter | solution.py:47
  323.1 84.7 %all-reduce = (f32[8,256]{1,0:T(8,128)S(1)}, f32[8,256]{1,0:T(8,128)S(1)}) all-reduce(f32[8,256]{1,0:T(8,128)} %reduce-scatter.5.cloned.1.call-done, f32[8,256]{1,0:T(8,128)} %reduce-scatter.3.cloned.1.call-done), channel_id=1, replica_groups=mesh['dp'=32,'mp'=16] {'mp'}, use_global_device_ids=true, to_apply=%region_5.6 | all-reduce | flops 4096 | bytes 32768 | tf_op jit(solution)/shard_map/psum | solution.py:48
  407.8 0.0 all-reduce.4.cloned.1.call-done
  407.8 0.0 copy-done
  407.8 1.2 fusion.129
  408.9 0.0 copy-done.1
  409.0 1.2 fusion.131
  410.1 1.2 fusion.133
  411.4 1.2 fusion.135
  412.6 0.0 copy-done.4
  412.6 9.8 %fusion.3 = bf16[8,1792]{1,0:T(8,128)(2,1)S(1)} fusion(s32[1792]{0:T(1024)S(1)} %fusion.205, s32[256]{0:T(256)S(1)} %and_select_fusion, bf16[2,8,1792]{2,1,0:T(8,128)(2,1)S(1)} %copy-done.4, f32[8,256]{1,0:T(8,128)S(1)} %fusion.131, f32[8,256]{1,0:T(8,128)S(1)} %fusion.129), kind=kOutput, calls=%fused_computation.69 | convolution fusion | flops 50067456 | bytes 81920 | tf_op jit(solution)/shard_map/dot_general | solution.py:61
  422.4 57.5 %all_gather.7 = bf16[256,1792]{1,0:T(8,128)(2,1)S(1)} all-gather(bf16[8,1792]{1,0:T(8,128)(2,1)S(1)} %fusion.3), channel_id=1, replica_groups=mesh['dp'=32,'mp'=16] {'dp'}, dimensions={0}, use_global_device_ids=true | all-gather | bytes 946176 | tf_op jit(solution)/shard_map/all_gather | solution.py:63
  479.9 9.8 %fusion.2 = bf16[8,1792]{1,0:T(8,128)(2,1)S(1)} fusion(s32[1792]{0:T(1024)S(1)} %fusion.191, s32[256]{0:T(256)S(1)} %and_select_fusion.2, bf16[2,8,1792]{2,1,0:T(8,128)(2,1)S(1)} %copy-done.4, f32[8,256]{1,0:T(8,128)S(1)} %fusion.135, f32[8,256]{1,0:T(8,128)S(1)} %fusion.133), kind=kOutput, calls=%fused_computation.68 | convolution fusion | flops 50067456 | bytes 81920 | tf_op jit(solution)/shard_map/dot_general | solution.py:61
  489.7 41.9 %all_gather.6 = bf16[256,1792]{1,0:T(8,128)(2,1)S(1)} all-gather(bf16[8,1792]{1,0:T(8,128)(2,1)S(1)} %fusion.2), channel_id=1, replica_groups=mesh['dp'=32,'mp'=16] {'dp'}, dimensions={0}, use_global_device_ids=true | all-gather | bytes 946176 | tf_op jit(solution)/shard_map/all_gather | solution.py:63
  531.6 0.6 pad_maximum_fusion.2
  532.2 0.6 pad_maximum_fusion.1
  532.8 1.4 pad_maximum_fusion
  (6 shorter events, 0.2 us)
Async XLA Ops:
  8.0 165.4 %reduce-scatter.5.cloned.1.call-start = ((), (), s32[]{:S(2)}) async-start(), calls=%async_computation.3 | async-start | bytes 270336 | tf_op jit(solution)/shard_map/reduce_scatter | solution.py:47
  10.1 13.0 %copy-start.3 = (bf16[1,2,256,1792]{3,2,1,0:T(8,128)(2,1)S(1)}, bf16[1,2,256,1792]{3,2,1,0:T(8,128)(2,1)}, u32[]{:S(2)}) copy-start(bf16[1,2,256,1792]{3,2,1,0:T(8,128)(2,1)} %param.6) | copy-start | bytes 5505028
  22.1 301.0 %reduce-scatter.3.cloned.1.call-start = ((), (), s32[]{:S(2)}) async-start(), calls=%async_computation.2 | async-start | bytes 270336 | tf_op jit(solution)/shard_map/reduce_scatter | solution.py:47
  23.1 11.1 %copy-start.2 = (s32[2]{0:T(128)S(1)}, s32[2]{0:T(128)}, u32[]{:S(2)}) copy-start(s32[2]{0:T(128)} %param.10) | copy-start | bytes 28
  33.8 374.0 %all-reduce.4.cloned.1.call-start = ((), (), s32[]{:S(2)}) async-start(), calls=%async_computation.4 | async-start | bytes 1048576 | tf_op jit(solution)/shard_map/psum | solution.py:45
  56.7 351.1 %copy-start = (f32[2,8,256]{2,1,0:T(8,128)S(1)}, f32[2,8,256]{2,1,0:T(8,128)}, u32[]{:S(2)}) copy-start(f32[2,8,256]{2,1,0:T(8,128)} %param.9) | copy-start | bytes 49156
  56.7 352.3 %copy-start.1 = (f32[2,8,256]{2,1,0:T(8,128)S(1)}, f32[2,8,256]{2,1,0:T(8,128)}, u32[]{:S(2)}) copy-start(f32[2,8,256]{2,1,0:T(8,128)} %param.8) | copy-start | bytes 49156
  56.7 355.9 %copy-start.4 = (bf16[2,8,1792]{2,1,0:T(8,128)(2,1)S(1)}, bf16[2,8,1792]{2,1,0:T(8,128)(2,1)}, u32[]{:S(2)}) copy-start(bf16[2,8,1792]{2,1,0:T(8,128)(2,1)} %param.7) | copy-start | bytes 172036
Sparse Core Ops, SparseCore 0:
  22.2 151.1 reduce-scatter.4
  176.1 146.8 reduce-scatter.2
Sparse Core Ops, SparseCore 1:
  77.6 199.6 all-reduce.3
where the time goes:
time: 550 us; the launch traced here: 542 us
  waiting for transfers between devices  246 us (45%)
  blocking collectives  184 us (33%)
  matrix products  88.2 us (16%)
  between operations  18.6 us (3%)
    reduce_scatter x2, waiting for transfers between devices, shards(): lax.psum_scatter(partial_value, 'dp', scatter_dimension=0, tiled=True)  246 us
    all_gather x2, blocking collectives, shards(): gathered.append(lax.all_gather(block, 'dp', axis=0, tiled=True))  99.4 us
    psum x1, blocking collectives, shards(): compressed = lax.psum(owned, 'mp')  84.7 us
    dot_general x4, matrix products, inner_rank(): lax.dot_general(left, right, (((1,), (1,)), ((), ())), preferred_element_...  63.8 us
    dot_general x2, matrix products, shards(): update = jnp.dot(direction, new_proj, preferred_element_type=jnp.float32)  19.6 us
  transfers between devices with their start and end apart: 3, of which 2 were waited for; matrix products, arithmetic and copies ran while one was open for 10% of the time, Pallas kernels for 0%

commit v1 on v0

--- a/solution.py
+++ b/solution.py
@@ -60,7 +60,11 @@
         direction = (moment / (jnp.sqrt(second) + 1e-08)).astype(jnp.bfloat16)
         update = jnp.dot(direction, new_proj, preferred_element_type=jnp.float32)
         block = (weights[layer_id].astype(jnp.float32) - 0.5 * update).astype(jnp.bfloat16)
-        gathered.append(lax.all_gather(block, "dp", axis=0, tiled=True))
+        gathered.append(
+            jnp.concatenate(
+                lax.all_to_all(jnp.stack([block] * lax.axis_size("dp")), "dp", 0, 0), axis=0
+            )
+        )
         firsts.append(moment)
         seconds.append(second)
     new_weights = jnp.stack(gathered)

time: 550 us -> 513 us (0.933)
  blocking collectives: 184 us -> 84.4 us
  waiting for transfers between devices: 246 us -> 282 us
  starting transfers between devices: 0.74 us -> 26.6 us
    all_gather x2 -> x0, blocking collectives: 99.4 us -> none  [shards(): gathered.append(lax.all_gather(block, 'dp', axis=0, tiled=True))]
    all_to_all x0 -> x2, waiting for transfers between devices: none -> 36.5 us  [shards(): lax.all_to_all(jnp.stack([block] * lax.axis_size('dp')), 'dp', 0, 0)]
    all_to_all x0 -> x2, starting transfers between devices: none -> 25.9 us  [shards(): lax.all_to_all(jnp.stack([block] * lax.axis_size('dp')), 'dp', 0, 0)]
  transfers between devices with their start and end apart: 3 -> 5, of which waited for: 2 -> 4; matrix products, arithmetic and copies ran while one was open for 10% -> 13% of each run, Pallas kernels for 0% -> 0%
where the time goes in v1:
time: 513 us; the launch traced here: 505 us
  waiting for transfers between devices  282 us (55%)
  matrix products  86.3 us (17%)
  blocking collectives  84.4 us (16%)
  starting transfers between devices  26.6 us (5%)
  between operations  18.6 us (4%)
    reduce_scatter x2, waiting for transfers between devices, shards(): lax.psum_scatter(partial_value, 'dp', scatter_dimension=0, tiled=True)  246 us
    psum x1, blocking collectives, shards(): compressed = lax.psum(owned, 'mp')  84.4 us
    dot_general x4, matrix products, inner_rank(): lax.dot_general(left, right, (((1,), (1,)), ((), ())), preferred_element_...  63.8 us
    all_to_all x2, waiting for transfers between devices, shards(): lax.all_to_all(jnp.stack([block] * lax.axis_size('dp')), 'dp', 0, 0)  36.5 us
    all_to_all x2, starting transfers between devices, shards(): lax.all_to_all(jnp.stack([block] * lax.axis_size('dp')), 'dp', 0, 0)  25.9 us
    dot_general x2, matrix products, shards(): update = jnp.dot(direction, new_proj, preferred_element_type=jnp.float32)  19.6 us
  transfers between devices with their start and end apart: 5, of which 4 were waited for; matrix products, arithmetic and copies ran while one was open for 13% of the time, Pallas kernels for 0%

profile of v1, /device:TPU:1, one launch (start us, length us, event | category | flops | bytes accessed | tf_op | source)
XLA Modules:
  0.0 505.2 jit_solution(9572615251793263686)
XLA Ops:
  8.0 0.0 reduce-scatter.5.cloned.1.call-start
  8.0 1.3 fusion.313
  10.1 0.0 copy-start.4
  10.1 11.9 %convolution_bitcast_fusion = f32[256,256]{1,0:T(8,128)} fusion(bf16[1,2,256,1792]{3,2,1,0:T(8,128)(2,1)} %param.6, s32[1792]{0:T(1024)S(1)} %fusion.205, s32[256]{0:T(256)S(1)} %and_select_fusion), kind=kOutput, calls=%fused_computation.211 | convolution fusion | flops 277544960 | bytes 1187840 | tf_op jit(solution)/shard_map/dot_general | solution.py:23
  22.1 0.0 reduce-scatter.5.cloned.1.call-update
  22.1 0.3 reduce-scatter.3.cloned.1.call-start
  23.1 0.0 copy-done.4
  23.1 0.0 copy-start.3
  23.1 10.6 %convolution_bitcast_fusion.1 = f32[256,256]{1,0:T(8,128)} fusion(bf16[1,2,256,1792]{3,2,1,0:T(8,128)(2,1)S(1)} %copy-done.4, s32[1792]{0:T(1024)S(1)} %fusion.191, s32[256]{0:T(256)S(1)} %and_select_fusion.2), kind=kOutput, calls=%fused_computation.212 | convolution fusion | flops 277544960 | bytes 1188864 | tf_op jit(solution)/shard_map/dot_general | solution.py:23
  33.7 0.0 reduce-scatter.3.cloned.1.call-update
  33.8 0.4 all-reduce.4.cloned.1.call-start
  34.2 0.0 copy-done.3
  34.2 0.6 fusion.312
  36.1 0.1 fusion.184
  36.3 20.4 %fusion.138 = f32[256,256]{1,0:T(8,128)} fusion(s32[1792]{0:T(1024)S(1)} %fusion.191, s32[256]{0:T(256)S(1)} %and_select_fusion.2, s32[1792]{0:T(1024)S(1)} %get-tuple-element.11, s32[256]{0:T(256)S(1)} %and_select_fusion.3), kind=kOutput, calls=%fused_computation.226 | convolution fusion | flops 320208896 | bytes 278528 | tf_op jit(solution)/shard_map/dot_general | solution.py:23
  56.7 0.0 copy-start.1
  56.7 0.0 copy-start.2
  56.7 0.0 copy-start.5
  56.7 20.8 %fusion.136 = f32[256,256]{1,0:T(8,128)} fusion(s32[1792]{0:T(1024)S(1)} %get-tuple-element.12, s32[256]{0:T(256)S(1)} %and_select_fusion.1, s32[1792]{0:T(1024)S(1)} %fusion.205, s32[256]{0:T(256)S(1)} %and_select_fusion), kind=kOutput, calls=%fused_computation.225 | convolution fusion | flops 320208896 | bytes 278528 | tf_op jit(solution)/shard_map/dot_general | solution.py:23
  77.5 0.0 all-reduce.4.cloned.1.call-update
  77.5 95.9 %reduce-scatter.5.cloned.1.call-done = f32[8,256]{1,0:T(8,128)} async-done(((f32[256,256]{1,0:T(8,128)}), f32[8,256]{1,0:T(8,128)}) %reduce-scatter.5.cloned.1.call-update) | async-done | bytes 8208 | tf_op jit(solution)/shard_map/reduce_scatter | solution.py:47
  173.5 149.9 %reduce-scatter.3.cloned.1.call-done = f32[8,256]{1,0:T(8,128)} async-done(((f32[256,256]{1,0:T(8,128)}), f32[8,256]{1,0:T(8,128)}) %reduce-scatter.3.cloned.1.call-update) | async-done | bytes 8208 | tf_op jit(solution)/shard_map/reduce_scatter | solution.py:47
  323.4 84.4 %all-reduce = (f32[8,256]{1,0:T(8,128)S(1)}, f32[8,256]{1,0:T(8,128)S(1)}) all-reduce(f32[8,256]{1,0:T(8,128)} %reduce-scatter.5.cloned.1.call-done, f32[8,256]{1,0:T(8,128)} %reduce-scatter.3.cloned.1.call-done), channel_id=1, replica_groups=mesh['dp'=32,'mp'=16] {'mp'}, use_global_device_ids=true, to_apply=%region_5.6 | all-reduce | flops 4096 | bytes 32768 | tf_op jit(solution)/shard_map/psum | solution.py:48
  407.8 0.0 all-reduce.4.cloned.1.call-done
  407.8 0.0 copy-done.1
  407.8 1.2 fusion.129
  408.9 0.0 copy-done.2
  409.0 1.2 fusion.131
  410.1 0.0 copy-done.5
  410.2 9.8 %fusion.3 = bf16[8,1792]{1,0:T(8,128)(2,1)S(1)} fusion(s32[1792]{0:T(1024)S(1)} %fusion.205, s32[256]{0:T(256)S(1)} %and_select_fusion, bf16[2,8,1792]{2,1,0:T(8,128)(2,1)S(1)} %copy-done.5, f32[8,256]{1,0:T(8,128)S(1)} %fusion.131, f32[8,256]{1,0:T(8,128)S(1)} %fusion.129), kind=kOutput, calls=%fused_computation.69 | convolution fusion | flops 50067456 | bytes 81920 | tf_op jit(solution)/shard_map/dot_general | solution.py:61
  420.0 0.0 copy-start
  420.0 1.0 stack.19
  421.0 21.1 %all-to-all-start.1 = ((bf16[32,8,1792]{2,1,0:T(8,128)(2,1)}), bf16[32,8,1792]{2,1,0:T(8,128)(2,1)S(1)}, u32[]{:S(2)}, u32[]{:S(2)}) async-start(bf16[32,8,1792]{2,1,0:T(8,128)(2,1)} %stack.19), calls=%async_computation.3 | async-start | bytes 1835008 | tf_op jit(solution)/shard_map/all_to_all | solution.py:65
  442.1 0.0 copy-done
  442.1 0.2 fusion.133
  442.3 0.3 fusion.135
  442.5 9.8 %fusion.2 = bf16[8,1792]{1,0:T(8,128)(2,1)S(1)} fusion(s32[1792]{0:T(1024)S(1)} %fusion.191, s32[256]{0:T(256)S(1)} %and_select_fusion.2, bf16[2,8,1792]{2,1,0:T(8,128)(2,1)S(1)} %copy-done.5, f32[8,256]{1,0:T(8,128)S(1)} %fusion.135, f32[8,256]{1,0:T(8,128)S(1)} %fusion.133), kind=kOutput, calls=%fused_computation.68 | convolution fusion | flops 50067456 | bytes 81920 | tf_op jit(solution)/shard_map/dot_general | solution.py:61
  452.4 13.7 %all-to-all-done.1 = bf16[32,8,1792]{2,1,0:T(8,128)(2,1)S(1)} async-done(((bf16[32,8,1792]{2,1,0:T(8,128)(2,1)}), bf16[32,8,1792]{2,1,0:T(8,128)(2,1)S(1)}, u32[]{:S(2)}, u32[]{:S(2)}) %all-to-all-start.1) | async-done | bytes 917536 | tf_op jit(solution)/shard_map/all_to_all | solution.py:65
  466.1 1.0 stack.18
  467.1 4.8 all-to-all-start
  471.9 0.6 pad_maximum_fusion.2
  472.5 0.6 pad_maximum_fusion.1
  473.1 22.8 %all-to-all-done = bf16[32,8,1792]{2,1,0:T(8,128)(2,1)S(1)} async-done(((bf16[32,8,1792]{2,1,0:T(8,128)(2,1)}), bf16[32,8,1792]{2,1,0:T(8,128)(2,1)S(1)}, u32[]{:S(2)}, u32[]{:S(2)}) %all-to-all-start) | async-done | bytes 917536 | tf_op jit(solution)/shard_map/all_to_all | solution.py:65
  496.0 1.4 pad_maximum_fusion
  (6 shorter events, 0.2 us)
Async XLA Ops:
  8.0 165.5 %reduce-scatter.5.cloned.1.call-start = ((), (), s32[]{:S(2)}) async-start(), calls=%async_computation.5 | async-start | bytes 270336 | tf_op jit(solution)/shard_map/reduce_scatter | solution.py:47
  10.1 13.0 %copy-start.4 = (bf16[1,2,256,1792]{3,2,1,0:T(8,128)(2,1)S(1)}, bf16[1,2,256,1792]{3,2,1,0:T(8,128)(2,1)}, u32[]{:S(2)}) copy-start(bf16[1,2,256,1792]{3,2,1,0:T(8,128)(2,1)} %param.6) | copy-start | bytes 5505028
  22.1 301.3 %reduce-scatter.3.cloned.1.call-start = ((), (), s32[]{:S(2)}) async-start(), calls=%async_computation.4 | async-start | bytes 270336 | tf_op jit(solution)/shard_map/reduce_scatter | solution.py:47
  23.1 11.1 %copy-start.3 = (s32[2]{0:T(128)S(1)}, s32[2]{0:T(128)}, u32[]{:S(2)}) copy-start(s32[2]{0:T(128)} %param.10) | copy-start | bytes 28
  33.8 374.0 %all-reduce.4.cloned.1.call-start = ((), (), s32[]{:S(2)}) async-start(), calls=%async_computation.6 | async-start | bytes 1048576 | tf_op jit(solution)/shard_map/psum | solution.py:45
  56.7 351.1 %copy-start.1 = (f32[2,8,256]{2,1,0:T(8,128)S(1)}, f32[2,8,256]{2,1,0:T(8,128)}, u32[]{:S(2)}) copy-start(f32[2,8,256]{2,1,0:T(8,128)} %param.9) | copy-start | bytes 49156
  56.7 352.3 %copy-start.2 = (f32[2,8,256]{2,1,0:T(8,128)S(1)}, f32[2,8,256]{2,1,0:T(8,128)}, u32[]{:S(2)}) copy-start(f32[2,8,256]{2,1,0:T(8,128)} %param.8) | copy-start | bytes 49156
  56.7 353.5 %copy-start.5 = (bf16[2,8,1792]{2,1,0:T(8,128)(2,1)S(1)}, bf16[2,8,1792]{2,1,0:T(8,128)(2,1)}, u32[]{:S(2)}) copy-start(bf16[2,8,1792]{2,1,0:T(8,128)(2,1)} %param.7) | copy-start | bytes 172036
  420.0 22.1 %copy-start = (f32[256,256]{1,0:T(8,128)S(1)}, f32[256,256]{1,0:T(8,128)}, u32[]{:S(2)}) copy-start(f32[256,256]{1,0:T(8,128)} %get-tuple-element.6) | copy-start | bytes 786436
  421.0 45.1 %all-to-all-start.1 = ((bf16[32,8,1792]{2,1,0:T(8,128)(2,1)}), bf16[32,8,1792]{2,1,0:T(8,128)(2,1)S(1)}, u32[]{:S(2)}, u32[]{:S(2)}) async-start(bf16[32,8,1792]{2,1,0:T(8,128)(2,1)} %stack.19), calls=%async_computation.3 | async-start | bytes 1835008 | tf_op jit(solution)/shard_map/all_to_all | solution.py:65
  467.1 28.9 %all-to-all-start = ((bf16[32,8,1792]{2,1,0:T(8,128)(2,1)}), bf16[32,8,1792]{2,1,0:T(8,128)(2,1)S(1)}, u32[]{:S(2)}, u32[]{:S(2)}) async-start(bf16[32,8,1792]{2,1,0:T(8,128)(2,1)} %stack.18), calls=%async_computation.1 | async-start | bytes 1835008 | tf_op jit(solution)/shard_map/all_to_all | solution.py:65
Sparse Core Ops, SparseCore 0:
  22.2 151.2 reduce-scatter.4
  176.2 147.0 reduce-scatter.2
Sparse Core Ops, SparseCore 1:
  77.6 199.4 all-reduce.3
